TPU v7x, 256 devices: a whole 4x4x8 slice. The times are simulated.
256 devices in a mesh: replica: 16 (over z_lo, x, core), tensor: 16 (over z_hi, y).
Axes of the slice: x: 4, y: 4, z: 8 (z_hi: 4, z_lo: 2; z = z_hi * 2 + z_lo), core: 2. Of those that a mesh axis runs over, the one named last changes fastest.
Arguments:
- grads: bfloat16 [16, 4096, 8192], P('replica', None, 'tensor'), may hold values from -100 to 100
- exponents: int32 [16, 64], P('replica', 'tensor'), may hold values from -4 to 1
- signs: int32 [4096], replicated, may hold values from 0 to 1
- weights: bfloat16 [4096, 8192], P(None, 'tensor'), may hold values from -3 to 3
Outputs:
- new_weights: bfloat16 [4096, 8192], P(None, 'tensor')
All inputs are finite; a program needn't handle non-finite values.
Results may differ from a plain program's by a relative error of at most 0.015.
Values may be sent and summed in bfloat16 or wider, within the bound.
A program may use at most 64 MiB of HBM per device.

v0:
```python
import functools

import jax
import jax.numpy as jnp
from jax import lax
from jax.experimental import pallas as pl
from jax.experimental.pallas import tpu as pltpu
from jax.sharding import PartitionSpec as P

COLS = 8192
OUTER, INNER = 16, 256
LANES, HALF = 128, 256
NA = 8
NG = 10
CHUNKS = [(0, 0), (0, 1), (1, 0), (1, 1)]
MESH = pl.DeviceIdType.MESH


def hadamard_values(values):
    values = list(values)
    step = 1
    while step < len(values):
        for i in range(len(values)):
            if not i & step:
                u, v = values[i], values[i + step]
                values[i], values[i + step] = u + v, u - v
        step *= 2
    return values


def inner_table():
    row = lax.broadcasted_iota(jnp.int32, (INNER, INNER), 0)
    col = lax.broadcasted_iota(jnp.int32, (INNER, INNER), 1)
    v = row & col
    v = v ^ (v >> 4)
    v = v ^ (v >> 2)
    v = v ^ (v >> 1)
    table = (1 - 2 * (v & 1)).astype(jnp.float32) * (1.0 / 64.0)
    return table.astype(jnp.bfloat16), row == col


def exchange(
    nt, exps_hbm, signs_hbm, grads, weights,
    gv, wv, hb, fac,
    exps, signs, g, y, qp, pr, p, rx1, s1, rz1, rz2, d, rx2, ov, ar, ld, ss, rs,
):
    f32, bf16 = jnp.float32, jnp.bfloat16
    r, t = lax.axis_index("replica"), lax.axis_index("tensor")
    z, x, c = r // 8, (r // 2) % 4, r % 2
    zh, yy = t // 4, t % 4
    oz, oc = 1 - z, 1 - c

    def dev(z=z, x=x, c=c, zh=zh, yy=yy):
        return (z * 8 + x * 2 + c, zh * 4 + yy)

    xo = {j: lax.rem(x + j, 4) for j in (1, 2, 3)}
    xpeer = {j: dev(x=xo[j]) for j in (1, 2, 3)}
    zpeer, cpeer, zcpeer = dev(z=oz), dev(c=oc), dev(z=oz, c=oc)
    ypeer = {j: dev(yy=lax.rem(yy + j, 4)) for j in (1, 2, 3)}
    zhpeer = {j: dev(zh=lax.rem(zh + j, 4)) for j in (1, 2, 3)}
    peers = [*xpeer.values(), zpeer, cpeer, zcpeer]
    if nt > 1:
        peers += [*ypeer.values(), *zhpeer.values()]
    barrier = pltpu.get_barrier_semaphore()
    for peer in peers:
        pl.semaphore_signal(barrier, inc=1, device_id=peer, device_id_type=MESH)

    n_local = 0

    def local(src, dst):
        nonlocal n_local
        copy = pltpu.make_async_copy(src, dst, ld.at[n_local])
        n_local += 1
        copy.start()
        return copy

    sent = []

    def remote(src, dst, peer):
        i = len(sent)
        copy = pltpu.make_async_remote_copy(
            src_ref=src, dst_ref=dst, send_sem=ss.at[i], recv_sem=rs.at[i], device_id=peer, device_id_type=MESH
        )
        copy.start()
        sent.append(copy)
        return copy

    small = [local(signs_hbm, signs), local(exps_hbm, exps)]
    loads = []
    for n, half in enumerate((oc, c)):
        cols = pl.ds(pl.multiple_of(half * HALF, HALF), HALF)
        loads.append([local(grads.at[pl.ds(a, 4), :, cols], g.at[n, pl.ds(a, 4)]) for a in range(0, OUTER, 4)])

    table, diagonal = inner_table()
    for copy in small:
        copy.wait()

    def sign_row(a):
        both = [signs[2 * a + i : 2 * a + i + 1, :] for i in (0, 1)]
        return (2 * jnp.concatenate(both, axis=1) - 1).astype(f32)

    def inner_pass(n):
        for a in range(OUTER):
            if a % 4 == 0:
                loads[n][a // 4].wait()
            y[a] = jnp.dot(table * sign_row(a).astype(bf16), g[n, a], preferred_element_type=f32)

    def outer_pass(k, half, dst, other=None):
        tile, part = CHUNKS[k]
        e = exps[0, 2 * half + tile]
        top = jnp.float32(0.0)
        for power in range(-4, 2):
            top = jnp.where(e == power, jnp.float32(4.0 * 2.0**power), top)
        lanes = pl.ds(tile * LANES, LANES)

        def one(i, carry):
            rows = pl.ds(pl.multiple_of(i * 32 + part * 16, 16), 16)
            values = hadamard_values([y[a, rows, lanes] for a in range(OUTER)])
            for a in range(OUTER):
                q = jnp.clip(values[a], -top, top).astype(bf16)
                at = (k, a, i // 2, i % 2)
                dst[at] = q if other is None else q + other[at]
            return carry

        lax.fori_loop(0, 8, one, 0)

    ks = range(len(CHUNKS))
    pair, a1x, a2z, a1z, a2x = {}, {}, {}, {}, {}
    inner_pass(0)
    for k in ks:
        outer_pass(k, oc, qp)
        if k == 0:
            pl.semaphore_wait(barrier, len(peers))
        pair[k] = remote(qp.at[k], pr.at[k], cpeer)
    inner_pass(1)

    for k in ks:
        pair[k].wait_recv()
        outer_pass(k, c, p, pr)
        a2z[k] = remote(p.at[k, pl.ds(NA, OUTER - NA), :, oz], rz2.at[k], zpeer)
        a1x[k] = [remote(p.at[k, pl.ds(0, NA), xo[j]], rx1.at[k, j - 1], xpeer[j]) for j in (2, 1, 3)]

    weight_load = local(weights, wv)
    for a in range(OUTER):
        signed = jnp.where(diagonal, jnp.broadcast_to(sign_row(a), (INNER, INNER)), 0.0).astype(bf16)
        hb[a] = jnp.dot(signed, table, preferred_element_type=f32).astype(bf16)

    for k in ks:
        for copy in a1x[k]:
            copy.wait_recv()

        for a in range(NA):
            total = p[k, a, x, oz].astype(f32)
            for j in range(3):
                total = total + rx1[k, j, a, oz].astype(f32)
            s1[k, a] = total.astype(bf16)
        a1z[k] = remote(s1.at[k], rz1.at[k], zpeer)
        a2z[k].wait_recv()
        for j in (2, 1, 3):
            for a in range(OUTER - NA):
                d[k, j - 1, a] = (p[k, NA + a, xo[j], z].astype(f32) + rz2[k, a, xo[j]].astype(f32)).astype(bf16)
        a2x[k] = [remote(d.at[k, j - 1], rx2.at[k, j - 1], xpeer[j]) for j in (2, 1, 3)]

    def place(k, a, x, h):
        tile, part = CHUNKS[k]
        return gv.at[2 * c + tile, a, x, h, pl.ds(part * 16, 16)]

    every, first, last = pl.ds(0, OUTER), pl.ds(0, OUTER // 2), pl.ds(OUTER // 2, OUTER // 2)
    ga, gb = pl.ds(0, NG), pl.ds(NG, OUTER - NG)
    ga_first, ga_last = pl.ds(0, NG // 2), pl.ds(NG // 2, NG - NG // 2)

    def pass_on(k, a, x, h, peer):
        return remote(place(k, a, x, h), place(k, a, x, h), peer)

    def to_core(k, x):
        tile, part = CHUNKS[k]
        block = gv.at[2 * c + tile, :, x, :, pl.ds(part * 16, 16)]
        return remote(block, block, cpeer)

    squares = jnp.zeros((16, LANES), f32)
    own_z, own_x, own_local = {}, {}, {}
    for k in ks:
        a1z[k].wait_recv()
        for copy in a2x[k]:
            copy.wait_recv()
        values = []
        for a in range(OUTER):
            total = p[k, a, x, z].astype(f32)
            if a < NA:
                for j in range(3):
                    total = total + rx1[k, j, a, z].astype(f32)
                total = total + rz1[k, a].astype(f32)
            else:
                total = total + rz2[k, a - NA, x].astype(f32)
                for j in range(3):
                    total = total + rx2[k, j, a - NA].astype(f32)
            squares = squares + total * total
            values.append(total)
        values = hadamard_values(values)
        for a in range(OUTER):
            ov[k, a] = values[a].astype(bf16)
        here = place(k, every, x, z)
        own_z[k] = remote(ov.at[k], here, zpeer)
        own_x[k] = {j: remote(ov.at[k], here, xpeer[j]) for j in (1, 3)}
        own_local[k] = local(ov.at[k], here)

    rounds = [(x, xpeer), (2 * z + c, {2: zpeer, 1: cpeer, 3: zcpeer})]
    if nt > 1:
        rounds = [(yy, ypeer), (zh, zhpeer)] + rounds
    ar_copies = []

    def ar_send(n, value):
        slot, to = rounds[n]
        ar[n, slot] = value
        ar_copies[:] = [remote(ar.at[n, slot], ar.at[n, slot], to[j]) for j in (2, 1, 3)]

    def ar_recv(n):
        for copy in ar_copies:
            copy.wait_recv()
        return (ar[n, 0] + ar[n, 1]) + (ar[n, 2] + ar[n, 3])

    ar_send(0, squares[:8] + squares[8:])
    left, right, far = xo[3], xo[1], xo[2]
    core = {k: [] for k in ks}
    relay_x, relay_z, on_x, on_x2, far_z = {}, {}, {}, {}, {}
    for k in ks:
        own_z[k].wait_recv()
        relay_x[k] = {j: pass_on(k, ga, x, oz, xpeer[j]) for j in (1, 3)}
        own_local[k].wait()
        core[k].append(to_core(k, x))
    if len(rounds) > 2:
        ar_send(1, ar_recv(0))
    for k in ks:
        own_x[k][1].wait_recv()
        on_x[k] = {1: pass_on(k, first, left, z, xpeer[1])}
        relay_z[k] = [pass_on(k, gb, left, z, zpeer)]
        own_x[k][3].wait_recv()
        on_x[k][3] = pass_on(k, last, right, z, xpeer[3])
        relay_z[k].append(pass_on(k, gb, right, z, zpeer))
    if len(rounds) > 2:
        ar_send(2, ar_recv(1))
    else:
        ar_send(1, ar_recv(0))
    for k in ks:
        relay_x[k][1].wait_recv()
        on_x2[k] = {1: pass_on(k, ga_first, left, oz, xpeer[1])}
        relay_x[k][3].wait_recv()
        on_x2[k][3] = pass_on(k, ga_last, right, oz, xpeer[3])
        on_x[k][3].wait_recv()
        far_z[k] = pass_on(k, gb, far, z, zpeer)
        relay_z[k][0].wait_recv()
        core[k].append(to_core(k, left))
        relay_z[k][1].wait_recv()
        core[k].append(to_core(k, right))
    if len(rounds) > 2:
        ar_send(3, ar_recv(2))
    for k in ks:
        on_x[k][1].wait_recv()
        on_x2[k][1].wait_recv()
        on_x2[k][3].wait_recv()
        far_z[k].wait_recv()
        core[k].append(to_core(k, far))
    total = ar_recv(len(rounds) - 1)
    total = jnp.sum(jnp.sum(total, axis=0, keepdims=True), axis=1, keepdims=True)
    factor = 0.5 / jnp.sqrt(total / (OUTER * INNER * COLS) + 1e-06)
    fac[...] = jnp.broadcast_to(factor, fac.shape)
    weight_load.wait()
    for copy in sent:
        copy.wait_send()
    for k in ks:
        for copy in core[k]:
            copy.wait_recv()


def finish(gv, wv, hb, fac, out, stage, sem):
    f32 = jnp.float32
    factor = fac[0:1, 0:1]
    copies = []
    for a in range(OUTER):
        block = jnp.concatenate([gv[i, a].reshape(INNER, LANES) for i in range(4)], axis=1)
        unrotated = jnp.dot(hb[a], block, preferred_element_type=f32)
        stage[a] = (wv[a].astype(f32) - factor * unrotated).astype(stage.dtype)
        copies.append(pltpu.make_async_copy(stage.at[a], out.at[a], sem.at[a]))
        copies[-1].start()
    for copy in copies:
        copy.wait()


def body(exponents, signs, grads, weights, nt):
    bf16, f32 = jnp.bfloat16, jnp.float32
    n_copies = 25 * len(CHUNKS) + 3 * (4 if nt > 1 else 2)
    vmem = pltpu.VMEM
    columns = grads.shape[-1]
    nk, na2 = len(CHUNKS), OUTER - NA
    chunk = (nk, OUTER, 4, 2, 16, LANES)
    any_, in_vmem = pl.BlockSpec(memory_space=pl.ANY), pl.BlockSpec(memory_space=pltpu.VMEM)
    gv, wv, hb, fac = pl.pallas_call(
        functools.partial(exchange, nt),
        out_shape=[
            vmem((4, OUTER, 4, 2, 32, LANES), bf16),
            vmem((OUTER, INNER, columns), bf16),
            vmem((OUTER, INNER, INNER), bf16),
            vmem((8, LANES), f32),
        ],
        in_specs=[any_] * 4,
        out_specs=[in_vmem] * 4,
        scratch_shapes=[
            pltpu.SMEM((1, 4), jnp.int32),
            vmem((32, LANES), jnp.int32),
            vmem((2, OUTER, INNER, HALF), bf16),
            vmem((OUTER, INNER, HALF), f32),
            vmem(chunk, bf16),
            vmem(chunk, bf16),
            vmem(chunk, bf16),
            vmem((nk, 3, NA, 2, 16, LANES), bf16),
            vmem((nk, NA, 16, LANES), bf16),
            vmem((nk, NA, 16, LANES), bf16),
            vmem((nk, na2, 4, 16, LANES), bf16),
            vmem((nk, 3, na2, 16, LANES), bf16),
            vmem((nk, 3, na2, 16, LANES), bf16),
            vmem((nk, OUTER, 16, LANES), bf16),
            vmem((4, 4, 8, LANES), f32),
            pltpu.SemaphoreType.DMA((16,)),
            pltpu.SemaphoreType.DMA((n_copies,)),
            pltpu.SemaphoreType.DMA((n_copies,)),
        ],
        compiler_params=pltpu.CompilerParams(
            collective_id=0, has_side_effects=True, vmem_limit_bytes=28 * 2**20
        ),
        name="average_step",
    )(
        pltpu.with_memory_space_constraint(exponents, pltpu.HBM),
        pltpu.with_memory_space_constraint(signs.reshape(32, LANES), pltpu.HBM),
        pltpu.with_memory_space_constraint(grads.reshape(OUTER, INNER, columns), pltpu.HBM),
        pltpu.with_memory_space_constraint(weights.reshape(OUTER, INNER, columns), pltpu.HBM),
    )
    out = pl.pallas_call(
        finish,
        out_shape=jax.ShapeDtypeStruct((OUTER, INNER, columns), bf16),
        in_specs=[in_vmem] * 4,
        out_specs=any_,
        scratch_shapes=[vmem((OUTER, INNER, columns), bf16), pltpu.SemaphoreType.DMA((OUTER,))],
        compiler_params=pltpu.CompilerParams(vmem_limit_bytes=24 * 2**20),
        name="finish_step",
    )(gv, wv, hb, fac)
    return out.reshape(OUTER * INNER, columns)


def solution(mesh):
    in_specs = (P("replica", None, "tensor"), P("replica", "tensor"), P(), P(None, "tensor"))
    nt = mesh.shape["tensor"]

    def step(grads, exponents, signs, weights):
        return body(exponents, signs, grads[0], weights, nt)

    return jax.shard_map(step, mesh=mesh, in_specs=in_specs, out_specs=P(None, "tensor"), check_vma=False)
```

profile of v0, /device:TPU:1, one launch (start us, length us, event | category | flops | bytes accessed | tf_op | source)
XLA Modules:
  0.0 51.6 jit_solution(9048018577904902172)
XLA Ops:
  0.0 49.3 %average_step.1 = (bf16[4,16,4,2,32,128]{5,4,3,2,1,0:T(8,128)(2,1)S(1)}, bf16[16,256,512]{2,1,0:T(8,128)(2,1)S(1)}, bf16[16,256,256]{2,1,0:T(8,128)(2,1)S(1)}, f32[8,128]{1,0:T(8,128)S(1)}) custom-call(s32[1,4]{1,0:T(1,128)} %exps_hbm.1, s32[32,128]{1,0:T(8,128)} %bitcast.6, bf16[16,256,512]{2,1,0:T(8,128)(2,1)} %bitcast.4, bf16[16,256,512]{2,1,0:T(8,128)(2,1)} %bitcast.5), custom_call_target="tpu_custom_call" | custom-call | tf_op jit(solution)/shard_map/average_step/pallas_call | solution.py:297
  49.3 2.4 %finish_step.1 = bf16[16,256,512]{2,1,0:T(8,128)(2,1)} custom-call(bf16[4,16,4,2,32,128]{5,4,3,2,1,0:T(8,128)(2,1)S(1)} %get-tuple-element.9.gv, bf16[16,256,512]{2,1,0:T(8,128)(2,1)S(1)} %get-tuple-element.10.wv, bf16[16,256,256]{2,1,0:T(8,128)(2,1)S(1)} %get-tuple-element.11.hb, f32[8,128]{1,0:T(8,128)S(1)} %get-tuple-element.12.fac), custom_call_target="tpu_custom_call" | custom-call | tf_op jit(solution)/shard_map/finish_step/pallas_call | solution.py:337
where the time goes:
time: 51.8 us; the launch traced here: 51.6 us
  Pallas kernels  51.6 us (100%)
    pallas_call x1, Pallas kernels, body(): pl.pallas_call(functools.partial(exchange, nt), out_shape=[vmem((4, OUTER...  49.3 us
    pallas_call x1, Pallas kernels, body(): pl.pallas_call(finish, out_shape=jax.ShapeDtypeStruct((OUTER, INNER, colu...  2.38 us

commit v1 on v0

v1 whole, which is shorter than its diff:
```python
import functools

import jax
import jax.numpy as jnp
from jax import lax
from jax.experimental import pallas as pl
from jax.experimental.pallas import tpu as pltpu
from jax.sharding import PartitionSpec as P

COLS = 8192
OUTER, INNER = 16, 256
LANES, HALF = 128, 256
NA = 9
NG = 10
CHUNKS = [(0, 0), (0, 1), (1, 0), (1, 1)]
ORDER = [
    "vp 0", "vp 3", "vp 2", "inner 1", "vp 1", "vo 0", "sz 0", "sd 0",
    "vo 2", "sz 2", "vo 3", "vo 1", "tables 0", "sz 3", "sd 2", "a2s1 0",
    "a1s2 0", "a1s2 3", "sz 1", "a1s2 2", "sd 3", "a2s1 2", "a1z 0", "sd 1",
    "a2s2 0", "a2s1 3", "a1z 3", "a1s2 1", "a1z 2", "a2s2 2", "a2s1 1", "a2s2 3",
    "fin 0", "a1z 1", "a2s2 1", "fin 2", "fin 3", "fin 1", "sum 0", "g1 0",
    "g1 3", "gc1 3", "g2f 0", "g2f 3", "g2f 2", "g2q 3", "g1 1", "g2q 0",
    "g1 2", "g2f 1", "sum 0", "drain 0", "g2q 2", "g2q 1", "g4 0", "g3 3",
    "g3 0", "g4 3", "g4 2", "g3 1", "gc1 2", "g3 2", "g4 1", "g5 0",
    "g5 2", "g5 3", "g6 0", "gc1 1", "g5 1", "gc1 0", "g6 3", "g6 2",
    "g6 1", "sum 0",
]
MESH = pl.DeviceIdType.MESH


def hadamard_values(values):
    values = list(values)
    step = 1
    while step < len(values):
        for i in range(len(values)):
            if not i & step:
                u, v = values[i], values[i + step]
                values[i], values[i + step] = u + v, u - v
        step *= 2
    return values


def inner_table():
    row = lax.broadcasted_iota(jnp.int32, (INNER, INNER), 0)
    col = lax.broadcasted_iota(jnp.int32, (INNER, INNER), 1)
    v = row & col
    v = v ^ (v >> 4)
    v = v ^ (v >> 2)
    v = v ^ (v >> 1)
    table = (1 - 2 * (v & 1)).astype(jnp.float32) * (1.0 / 64.0)
    return table.astype(jnp.bfloat16), row == col


def exchange(
    nt, exps_hbm, signs_hbm, grads, weights,
    gv, wv, hb, fac,
    exps, signs, g, y, qp, pr, p, rt, rd, rx, t1, s1, rz1, rz2, d, ru, re, rv, t2, ov, ar, ld, ss, rs, entered,
):
    f32, bf16 = jnp.float32, jnp.bfloat16
    r, t = lax.axis_index("replica"), lax.axis_index("tensor")
    z, x, c = r // 8, (r // 2) % 4, r % 2
    zh, yy = t // 4, t % 4
    oz, oc = 1 - z, 1 - c

    def dev(z=z, x=x, c=c, zh=zh, yy=yy):
        return (z * 8 + x * 2 + c, zh * 4 + yy)

    xo = {j: lax.rem(x + j, 4) for j in (1, 2, 3)}
    xpeer = {j: dev(x=xo[j]) for j in (1, 2, 3)}
    zpeer, cpeer, zcpeer = dev(z=oz), dev(c=oc), dev(z=oz, c=oc)
    rounds = [(x, list(xpeer.values())), (2 * z + c, [zpeer, cpeer, zcpeer])]
    later = {}
    if nt > 1:
        turn = {j: (xo[j], lax.rem(yy + j, 4)) for j in (1, 2, 3)}
        turn[0] = (x, yy)
        plane = [dev(x=turn[i][0], yy=turn[j][1]) for i in range(4) for j in range(4) if i or j]
        later = {j: [] for j in (1, 2, 3)}
        for j in later:
            there = lax.rem(zh + j, 4)
            later[j] = [dev(zh=there, z=u, c=w_) for u in (z, oz) for w_ in (c, oc)]
        across = [peer for j in later for peer in later[j]]
        rounds = [(yy * 4 + x, plane), (zh * 4 + rounds[1][0], rounds[1][1] + across)]
    peers = rounds[0][1] + [zpeer, cpeer, zcpeer]
    barrier = pltpu.get_barrier_semaphore()
    for peer in peers:
        pl.semaphore_signal(barrier, inc=1, device_id=peer, device_id_type=MESH)
    for j in later:

        @pl.when(zh + j < 4)
        def greet_later(j=j):
            for peer in later[j]:
                pl.semaphore_signal(barrier, inc=1, device_id=peer, device_id_type=MESH)

    def enter():
        pl.semaphore_wait(barrier, len(peers) + (4 * zh if nt > 1 else 0))
        for j in later:

            @pl.when(zh + j >= 4)
            def answer_earlier(j=j):
                for peer in later[j]:
                    pl.semaphore_signal(entered, inc=1, device_id=peer, device_id_type=MESH)

    def await_later():
        if nt > 1:

            @pl.when(zh < 3)
            def _():
                pl.semaphore_wait(entered, 12 - 4 * zh)

    n_local = 0

    def local(src, dst):
        nonlocal n_local
        copy = pltpu.make_async_copy(src, dst, ld.at[n_local])
        n_local += 1
        copy.start()
        return copy

    sent = []

    def remote(src, dst, peer):
        i = len(sent)
        copy = pltpu.make_async_remote_copy(
            src_ref=src, dst_ref=dst, send_sem=ss.at[i], recv_sem=rs.at[i], device_id=peer, device_id_type=MESH
        )
        copy.start()
        sent.append(copy)
        return copy

    small = [local(signs_hbm, signs), local(exps_hbm, exps)]
    loads = []
    for n, half in enumerate((oc, c)):
        cols = pl.ds(pl.multiple_of(half * HALF, HALF), HALF)
        loads.append([local(grads.at[pl.ds(a, 4), :, cols], g.at[n, pl.ds(a, 4)]) for a in range(0, OUTER, 4)])

    table, diagonal = inner_table()
    for copy in small:
        copy.wait()

    def sign_row(a):
        both = [signs[2 * a + i : 2 * a + i + 1, :] for i in (0, 1)]
        return (2 * jnp.concatenate(both, axis=1) - 1).astype(f32)

    def inner_pass(n):
        for a in range(OUTER):
            if a % 4 == 0:
                loads[n][a // 4].wait()
            y[n, a] = jnp.dot(table * sign_row(a).astype(bf16), g[n, a], preferred_element_type=f32)

    def outer_pass(k, n, half, dst, other=None):
        tile, part = CHUNKS[k]
        e = exps[0, 2 * half + tile]
        top = jnp.float32(0.0)
        for power in range(-4, 2):
            top = jnp.where(e == power, jnp.float32(4.0 * 2.0**power), top)
        lanes = pl.ds(tile * LANES, LANES)

        def one(i, carry):
            rows = pl.ds(pl.multiple_of(i * 32 + part * 16, 16), 16)
            values = hadamard_values([y[n, a, rows, lanes] for a in range(OUTER)])
            for a in range(OUTER):
                q = jnp.clip(values[a], -top, top).astype(bf16)
                at = (k, a, i // 2, i % 2)
                dst[at] = q if other is None else q + other[at]
            return carry

        lax.fori_loop(0, 8, one, 0)

    inner_pass(0)
    ks = range(len(CHUNKS))
    n2 = OUTER - NA
    left, right, far = xo[3], xo[1], xo[2]
    to_right, to_left = xpeer[1], xpeer[3]
    c_ = {}
    a1 = pl.ds(0, NA)

    def split(k):
        n = (n2 + 1 - k % 2) // 2
        return n, pl.ds(0, n), pl.ds(n, n2 - n)

    def wait(k, *names):
        for name in names:
            c_[name, k].wait_recv()

    def wide(ref, *at):
        return ref[at].astype(f32)

    def other_columns(k):
        outer_pass(k, 0, oc, qp)
        if k == 0:
            enter()
        c_["pair", k] = remote(qp.at[k], pr.at[k], cpeer)

    def own_columns(k):
        wait(k, "pair")
        outer_pass(k, 1, c, p, pr)
        c_["tR", k] = remote(p.at[k, a1, far, z], rt.at[k, 0], to_right)
        c_["tL", k] = remote(p.at[k, a1, far, oz], rt.at[k, 1], to_left)

    def z_first(k):
        c_["z2", k] = remote(p.at[k, pl.ds(NA, n2), :, oz], rz2.at[k], zpeer)

    def x_direct(k):
        c_["dR", k] = remote(p.at[k, a1, right, oz], rd.at[k, 0], to_right)
        c_["dL", k] = remote(p.at[k, a1, left, z], rd.at[k, 1], to_left)

    def x_second(k):
        wait(k, "tR")
        for a in range(NA):
            t1[k, 0, a] = rt[k, 0, a] + p[k, a, right, z]
        c_["xR", k] = remote(t1.at[k, 0], rx.at[k, 0], to_right)
        wait(k, "tL")
        for a in range(NA):
            t1[k, 1, a] = rt[k, 1, a] + p[k, a, left, oz]
        c_["xL", k] = remote(t1.at[k, 1], rx.at[k, 1], to_left)

    def z_then_x(k):
        wait(k, "z2")
        n, upper, lower = split(k)
        for j in (2, 1, 3):
            for a in range(n2):
                d[k, j - 1, a] = p[k, NA + a, xo[j], z] + rz2[k, a, xo[j]]
            if j == 2:
                c_["uR", k] = remote(d.at[k, 1, upper], ru.at[k, upper], to_right)
                c_["uL", k] = remote(d.at[k, 1, lower], ru.at[k, lower], to_left)
        c_["eR", k] = remote(d.at[k, 0, lower], re.at[k, lower], to_right)
        c_["eL", k] = remote(d.at[k, 2, upper], re.at[k, upper], to_left)

    def x_then_z(k):
        wait(k, "dR", "xL")
        for a in range(NA):
            s1[k, a] = (wide(p, k, a, x, oz) + wide(rd, k, 0, a) + wide(rx, k, 1, a)).astype(bf16)
        c_["z1", k] = remote(s1.at[k], rz1.at[k], zpeer)

    def x_second_after_z(k):
        n, upper, lower = split(k)
        wait(k, "uR")
        for a in range(n):
            t2[k, a] = ru[k, a] + d[k, 0, a]
        c_["vR", k] = remote(t2.at[k, upper], rv.at[k, upper], to_right)
        wait(k, "uL")
        for a in range(n, n2):
            t2[k, a] = ru[k, a] + d[k, 2, a]
        c_["vL", k] = remote(t2.at[k, lower], rv.at[k, lower], to_left)

    def place(k, a, x, h):
        tile, part = CHUNKS[k]
        return gv.at[2 * c + tile, a, x, h, pl.ds(part * 16, 16)]

    every, first, last = pl.ds(0, OUTER), pl.ds(0, OUTER // 2), pl.ds(OUTER // 2, OUTER // 2)
    ga, gb = pl.ds(0, NG), pl.ds(NG, OUTER - NG)
    ga_first, ga_last = pl.ds(0, NG // 2), pl.ds(NG // 2, NG - NG // 2)

    def pass_on(name, k, a, x, h, peer):
        c_[name, k] = remote(place(k, a, x, h), place(k, a, x, h), peer)

    def to_core(name, k, x):
        tile, part = CHUNKS[k]
        block = gv.at[2 * c + tile, :, x, :, pl.ds(part * 16, 16)]
        c_[name, k] = remote(block, block, cpeer)

    squares = []

    def own_rows(k):
        wait(k, "dL", "xR", "eR", "eL", "vR", "vL", "z1")
        values, square = [], jnp.zeros((16, LANES), f32)
        for a in range(OUTER):
            total = wide(p, k, a, x, z)
            if a < NA:
                total = total + wide(rd, k, 1, a) + wide(rx, k, 0, a) + wide(rz1, k, a)
            else:
                total = total + wide(rz2, k, a - NA, x) + wide(re, k, a - NA) + wide(rv, k, a - NA)
            square = square + total * total
            values.append(total)
        squares.append(square)
        values = hadamard_values(values)
        for a in range(OUTER):
            ov[k, a] = values[a].astype(bf16)
        here = place(k, every, x, z)
        c_["oz", k] = remote(ov.at[k], here, zpeer)
        c_["oR", k] = remote(ov.at[k], here, to_right)
        c_["oL", k] = remote(ov.at[k], here, to_left)
        c_["own", k] = local(ov.at[k], here)

    def gather_z(k):
        wait(k, "oz")
        pass_on("rR", k, ga, x, oz, to_right)
        pass_on("rL", k, ga, x, oz, to_left)

    def core_own(k):
        c_["own", k].wait()
        to_core("c1", k, x)

    def gather_x(k):
        wait(k, "oR")
        pass_on("fR", k, first, left, z, to_right)
        wait(k, "oL")
        pass_on("fL", k, last, right, z, to_left)

    def gather_x_z(k):
        pass_on("qa", k, gb, left, z, zpeer)
        pass_on("qb", k, gb, right, z, zpeer)

    def gather_x_second(k):
        wait(k, "rR")
        pass_on("hR", k, ga_first, left, oz, to_right)
        wait(k, "rL")
        pass_on("hL", k, ga_last, right, oz, to_left)

    def gather_far_z(k):
        wait(k, "fL")
        pass_on("qc", k, gb, far, z, zpeer)

    def core_near(k):
        wait(k, "qa")
        to_core("c2", k, left)
        wait(k, "qb")
        to_core("c3", k, right)

    def core_far(k):
        wait(k, "fR", "hR", "hL", "qc")
        to_core("c4", k, far)

    ar_copies = []
    ar_round = 0

    def sum_round():
        nonlocal ar_round
        n = ar_round
        ar_round += 1
        if n == 0:
            total = functools.reduce(lambda u, v: u + v, squares)
            total = total[:8] + total[8:]
        else:
            for copy in ar_copies:
                copy.wait_recv()
            slots = len(rounds[n - 1][1]) + 1
            total = functools.reduce(lambda u, v: u + v, [ar[n - 1, i] for i in range(slots)])
        if n == len(rounds):
            return total
        slot, to = rounds[n]
        ar[n, slot] = total
        if n == 1:
            await_later()
        ar_copies[:] = [remote(ar.at[n, slot], ar.at[n, slot], peer) for peer in to]
        return None

    drained = 0

    def drain(upto):
        nonlocal drained
        for copy in sent[drained:upto]:
            copy.wait_send()
        drained = upto

    steps = dict(
        vp=other_columns,
        vo=own_columns,
        sd=x_direct,
        sz=z_first,
        a1s2=x_second,
        a2s1=z_then_x,
        a1z=x_then_z,
        a2s2=x_second_after_z,
        fin=own_rows,
        g1=gather_z,
        gc1=core_own,
        g2f=gather_x,
        g2q=gather_x_z,
        g3=gather_x_second,
        g4=gather_far_z,
        g5=core_near,
        g6=core_far,
    )
    total, weight_load, scattered = None, None, 0
    for step in ORDER:
        name, k = step.split()
        if name == "inner":
            inner_pass(1)
        elif name == "tables":
            weight_load = local(weights, wv)
            for a in range(OUTER):
                signed = jnp.where(diagonal, jnp.broadcast_to(sign_row(a), (INNER, INNER)), 0.0).astype(bf16)
                hb[a] = jnp.dot(signed, table, preferred_element_type=f32).astype(bf16)
        elif name == "sum":
            scattered = scattered or len(sent)
            got = sum_round()
            total = total if got is None else got
        elif name == "drain":
            drain(scattered)
        else:
            steps[name](int(k))

    total = jnp.sum(jnp.sum(total, axis=0, keepdims=True), axis=1, keepdims=True)
    factor = 0.5 / jnp.sqrt(total / (OUTER * INNER * COLS) + 1e-06)
    fac[...] = jnp.broadcast_to(factor, fac.shape)
    weight_load.wait()
    drain(len(sent))
    for k in ks:
        wait(k, "c1", "c2", "c3", "c4")


def finish(gv, wv, hb, fac, out, stage, sem):
    f32 = jnp.float32
    factor = fac[0:1, 0:1]
    copies = []
    for a in range(OUTER):
        block = jnp.concatenate([gv[i, a].reshape(INNER, LANES) for i in range(4)], axis=1)
        unrotated = jnp.dot(hb[a], block, preferred_element_type=f32)
        stage[a] = (wv[a].astype(f32) - factor * unrotated).astype(stage.dtype)
        copies.append(pltpu.make_async_copy(stage.at[a], out.at[a], sem.at[a]))
        copies[-1].start()
    for copy in copies:
        copy.wait()


def body(exponents, signs, grads, weights, nt):
    bf16, f32 = jnp.bfloat16, jnp.float32
    n_copies = 31 * len(CHUNKS) + 2 * (15 if nt > 1 else 3)
    vmem = pltpu.VMEM
    columns = grads.shape[-1]
    nk, na2 = len(CHUNKS), OUTER - NA
    chunk = (nk, OUTER, 4, 2, 16, LANES)
    any_, in_vmem = pl.BlockSpec(memory_space=pl.ANY), pl.BlockSpec(memory_space=pltpu.VMEM)
    gv, wv, hb, fac = pl.pallas_call(
        functools.partial(exchange, nt),
        out_shape=[
            vmem((4, OUTER, 4, 2, 32, LANES), bf16),
            vmem((OUTER, INNER, columns), bf16),
            vmem((OUTER, INNER, INNER), bf16),
            vmem((8, LANES), f32),
        ],
        in_specs=[any_] * 4,
        out_specs=[in_vmem] * 4,
        scratch_shapes=[
            pltpu.SMEM((1, 4), jnp.int32),
            vmem((32, LANES), jnp.int32),
            vmem((2, OUTER, INNER, HALF), bf16),
            vmem((2, OUTER, INNER, HALF), f32),
            vmem(chunk, bf16),
            vmem(chunk, bf16),
            vmem(chunk, bf16),
            vmem((nk, 2, NA, 16, LANES), bf16),
            vmem((nk, 2, NA, 16, LANES), bf16),
            vmem((nk, 2, NA, 16, LANES), bf16),
            vmem((nk, 2, NA, 16, LANES), bf16),
            vmem((nk, NA, 16, LANES), bf16),
            vmem((nk, NA, 16, LANES), bf16),
            vmem((nk, na2, 4, 16, LANES), bf16),
            vmem((nk, 3, na2, 16, LANES), bf16),
            vmem((nk, na2, 16, LANES), bf16),
            vmem((nk, na2, 16, LANES), bf16),
            vmem((nk, na2, 16, LANES), bf16),
            vmem((nk, na2, 16, LANES), bf16),
            vmem((nk, OUTER, 16, LANES), bf16),
            vmem((2, 16, 8, LANES), f32),
            pltpu.SemaphoreType.DMA((16,)),
            pltpu.SemaphoreType.DMA((n_copies,)),
            pltpu.SemaphoreType.DMA((n_copies,)),
            pltpu.SemaphoreType.REGULAR,
        ],
        compiler_params=pltpu.CompilerParams(
            collective_id=0, has_side_effects=True, vmem_limit_bytes=30 * 2**20
        ),
        name="average_step",
    )(
        pltpu.with_memory_space_constraint(exponents, pltpu.HBM),
        pltpu.with_memory_space_constraint(signs.reshape(32, LANES), pltpu.HBM),
        pltpu.with_memory_space_constraint(grads.reshape(OUTER, INNER, columns), pltpu.HBM),
        pltpu.with_memory_space_constraint(weights.reshape(OUTER, INNER, columns), pltpu.HBM),
    )
    out = pl.pallas_call(
        finish,
        out_shape=jax.ShapeDtypeStruct((OUTER, INNER, columns), bf16),
        in_specs=[in_vmem] * 4,
        out_specs=any_,
        scratch_shapes=[vmem((OUTER, INNER, columns), bf16), pltpu.SemaphoreType.DMA((OUTER,))],
        compiler_params=pltpu.CompilerParams(vmem_limit_bytes=24 * 2**20),
        name="finish_step",
    )(gv, wv, hb, fac)
    return out.reshape(OUTER * INNER, columns)


def solution(mesh):
    in_specs = (P("replica", None, "tensor"), P("replica", "tensor"), P(), P(None, "tensor"))
    nt = mesh.shape["tensor"]

    def step(grads, exponents, signs, weights):
        return body(exponents, signs, grads[0], weights, nt)

    return jax.shard_map(step, mesh=mesh, in_specs=in_specs, out_specs=P(None, "tensor"), check_vma=False)
```

time: 51.8 us -> 49.6 us (0.958)
  Pallas kernels: 51.6 us -> 49.4 us
    pallas_call x1, Pallas kernels: 49.3 us -> 47 us  [body(): pl.pallas_call(functools.partial(exchange, nt), out_shape=[vmem((4, OUTER...]
where the time goes in v1:
time: 49.6 us; the launch traced here: 49.4 us
  Pallas kernels  49.4 us (100%)
    pallas_call x1, Pallas kernels, body(): pl.pallas_call(functools.partial(exchange, nt), out_shape=[vmem((4, OUTER...  47 us
    pallas_call x1, Pallas kernels, body(): pl.pallas_call(finish, out_shape=jax.ShapeDtypeStruct((OUTER, INNER, colu...  2.38 us

profile of v1, /device:TPU:1, one launch (start us, length us, event | category | flops | bytes accessed | tf_op | source)
XLA Modules:
  0.0 49.4 jit_solution(11087952822879977816)
XLA Ops:
  0.0 47.0 %average_step.1 = (bf16[4,16,4,2,32,128]{5,4,3,2,1,0:T(8,128)(2,1)S(1)}, bf16[16,256,512]{2,1,0:T(8,128)(2,1)S(1)}, bf16[16,256,256]{2,1,0:T(8,128)(2,1)S(1)}, f32[8,128]{1,0:T(8,128)S(1)}) custom-call(s32[1,4]{1,0:T(1,128)} %exps_hbm.1, s32[32,128]{1,0:T(8,128)} %bitcast.6, bf16[16,256,512]{2,1,0:T(8,128)(2,1)} %bitcast.4, bf16[16,256,512]{2,1,0:T(8,128)(2,1)} %bitcast.5), custom_call_target="tpu_custom_call" | custom-call | tf_op jit(solution)/shard_map/average_step/pallas_call | solution.py:425
  47.0 2.4 %finish_step.1 = bf16[16,256,512]{2,1,0:T(8,128)(2,1)} custom-call(bf16[4,16,4,2,32,128]{5,4,3,2,1,0:T(8,128)(2,1)S(1)} %get-tuple-element.9.gv, bf16[16,256,512]{2,1,0:T(8,128)(2,1)S(1)} %get-tuple-element.10.wv, bf16[16,256,256]{2,1,0:T(8,128)(2,1)S(1)} %get-tuple-element.11.hb, f32[8,128]{1,0:T(8,128)S(1)} %get-tuple-element.12.fac), custom_call_target="tpu_custom_call" | custom-call | tf_op jit(solution)/shard_map/finish_step/pallas_call | solution.py:472

commit v2 on v1

--- a/solution.py
+++ b/solution.py
@@ -18,12 +18,12 @@
     "vo 2", "sz 2", "vo 3", "vo 1", "tables 0", "sz 3", "sd 2", "a2s1 0",
     "a1s2 0", "a1s2 3", "sz 1", "a1s2 2", "sd 3", "a2s1 2", "a1z 0", "sd 1",
     "a2s2 0", "a2s1 3", "a1z 3", "a1s2 1", "a1z 2", "a2s2 2", "a2s1 1", "a2s2 3",
-    "fin 0", "a1z 1", "a2s2 1", "fin 2", "fin 3", "fin 1", "sum 0", "g1 0",
-    "g1 3", "gc1 3", "g2f 0", "g2f 3", "g2f 2", "g2q 3", "g1 1", "g2q 0",
-    "g1 2", "g2f 1", "sum 0", "drain 0", "g2q 2", "g2q 1", "g4 0", "g3 3",
-    "g3 0", "g4 3", "g4 2", "g3 1", "gc1 2", "g3 2", "g4 1", "g5 0",
-    "g5 2", "g5 3", "g6 0", "gc1 1", "g5 1", "gc1 0", "g6 3", "g6 2",
-    "g6 1", "sum 0",
+    "fin 0", "a1z 1", "a2s2 1", "fin 2", "fin 3", "drain 0", "fin 1", "sum 0",
+    "g1 0", "g1 3", "gc1 3", "g2f 0", "g2f 3", "g2f 2", "g2q 3", "g1 1",
+    "g2q 0", "g1 2", "g2f 1", "sum 0", "g2q 2", "g2q 1", "g4 0", "g3 3",
+    "g3 0", "g4 3", "drain 0", "g4 2", "g3 1", "gc1 2", "g3 2", "g4 1",
+    "g5 0", "g5 2", "g5 3", "drain 0", "g6 0", "gc1 1", "g5 1", "gc1 0",
+    "g6 3", "g6 2", "drain 0", "g6 1", "sum 0",
 ]
 MESH = pl.DeviceIdType.MESH
 
@@ -80,33 +80,6 @@
             later[j] = [dev(zh=there, z=u, c=w_) for u in (z, oz) for w_ in (c, oc)]
         across = [peer for j in later for peer in later[j]]
         rounds = [(yy * 4 + x, plane), (zh * 4 + rounds[1][0], rounds[1][1] + across)]
-    peers = rounds[0][1] + [zpeer, cpeer, zcpeer]
-    barrier = pltpu.get_barrier_semaphore()
-    for peer in peers:
-        pl.semaphore_signal(barrier, inc=1, device_id=peer, device_id_type=MESH)
-    for j in later:
-
-        @pl.when(zh + j < 4)
-        def greet_later(j=j):
-            for peer in later[j]:
-                pl.semaphore_signal(barrier, inc=1, device_id=peer, device_id_type=MESH)
-
-    def enter():
-        pl.semaphore_wait(barrier, len(peers) + (4 * zh if nt > 1 else 0))
-        for j in later:
-
-            @pl.when(zh + j >= 4)
-            def answer_earlier(j=j):
-                for peer in later[j]:
-                    pl.semaphore_signal(entered, inc=1, device_id=peer, device_id_type=MESH)
-
-    def await_later():
-        if nt > 1:
-
-            @pl.when(zh < 3)
-            def _():
-                pl.semaphore_wait(entered, 12 - 4 * zh)
-
     n_local = 0
 
     def local(src, dst):
@@ -115,6 +88,40 @@
         n_local += 1
         copy.start()
         return copy
+
+    loads = []
+    for n, half in enumerate((oc, c)):
+        cols = pl.ds(pl.multiple_of(half * HALF, HALF), HALF)
+        loads.append([local(grads.at[pl.ds(a, 4), :, cols], g.at[n, pl.ds(a, 4)]) for a in range(0, OUTER, 4)])
+        if n == 0:
+            small = [local(signs_hbm, signs), local(exps_hbm, exps)]
+
+    peers = rounds[0][1] + [zpeer, cpeer, zcpeer]
+    barrier = pltpu.get_barrier_semaphore()
+    for peer in peers:
+        pl.semaphore_signal(barrier, inc=1, device_id=peer, device_id_type=MESH)
+    for j in later:
+
+        @pl.when(zh + j < 4)
+        def greet_later(j=j):
+            for peer in later[j]:
+                pl.semaphore_signal(barrier, inc=1, device_id=peer, device_id_type=MESH)
+
+    def enter():
+        pl.semaphore_wait(barrier, len(peers) + (4 * zh if nt > 1 else 0))
+        for j in later:
+
+            @pl.when(zh + j >= 4)
+            def answer_earlier(j=j):
+                for peer in later[j]:
+                    pl.semaphore_signal(entered, inc=1, device_id=peer, device_id_type=MESH)
+
+    def await_later():
+        if nt > 1:
+
+            @pl.when(zh < 3)
+            def _():
+                pl.semaphore_wait(entered, 12 - 4 * zh)
 
     sent = []
 
@@ -126,12 +133,6 @@
         copy.start()
         sent.append(copy)
         return copy
-
-    small = [local(signs_hbm, signs), local(exps_hbm, exps)]
-    loads = []
-    for n, half in enumerate((oc, c)):
-        cols = pl.ds(pl.multiple_of(half * HALF, HALF), HALF)
-        loads.append([local(grads.at[pl.ds(a, 4), :, cols], g.at[n, pl.ds(a, 4)]) for a in range(0, OUTER, 4)])
 
     table, diagonal = inner_table()
     for copy in small:
@@ -330,7 +331,7 @@
         ar_round += 1
         if n == 0:
             total = functools.reduce(lambda u, v: u + v, squares)
-            total = total[:8] + total[8:]
+            total = jnp.sum(total, axis=0, keepdims=True)
         else:
             for copy in ar_copies:
                 copy.wait_recv()
@@ -372,7 +373,7 @@
         g5=core_near,
         g6=core_far,
     )
-    total, weight_load, scattered = None, None, 0
+    total, weight_load, mark = None, None, 0
     for step in ORDER:
         name, k = step.split()
         if name == "inner":
@@ -383,15 +384,15 @@
                 signed = jnp.where(diagonal, jnp.broadcast_to(sign_row(a), (INNER, INNER)), 0.0).astype(bf16)
                 hb[a] = jnp.dot(signed, table, preferred_element_type=f32).astype(bf16)
         elif name == "sum":
-            scattered = scattered or len(sent)
             got = sum_round()
             total = total if got is None else got
         elif name == "drain":
-            drain(scattered)
+            drain(mark)
+            mark = len(sent)
         else:
             steps[name](int(k))
 
-    total = jnp.sum(jnp.sum(total, axis=0, keepdims=True), axis=1, keepdims=True)
+    total = jnp.sum(total, axis=1, keepdims=True)
     factor = 0.5 / jnp.sqrt(total / (OUTER * INNER * COLS) + 1e-06)
     fac[...] = jnp.broadcast_to(factor, fac.shape)
     weight_load.wait()
@@ -453,7 +454,7 @@
             vmem((nk, na2, 16, LANES), bf16),
             vmem((nk, na2, 16, LANES), bf16),
             vmem((nk, OUTER, 16, LANES), bf16),
-            vmem((2, 16, 8, LANES), f32),
+            vmem((2, 16, 1, LANES), f32),
             pltpu.SemaphoreType.DMA((16,)),
             pltpu.SemaphoreType.DMA((n_copies,)),
             pltpu.SemaphoreType.DMA((n_copies,)),

time: 49.6 us -> 48.5 us (0.978)
  Pallas kernels: 49.4 us -> 48.4 us
    pallas_call x1, Pallas kernels: 47 us -> 46 us  [body(): pl.pallas_call(functools.partial(exchange, nt), out_shape=[vmem((4, OUTER...]
where the time goes in v2:
time: 48.5 us; the launch traced here: 48.4 us
  Pallas kernels  48.4 us (100%)
    pallas_call x1, Pallas kernels, body(): pl.pallas_call(functools.partial(exchange, nt), out_shape=[vmem((4, OUTER...  46 us
    pallas_call x1, Pallas kernels, body(): pl.pallas_call(finish, out_shape=jax.ShapeDtypeStruct((OUTER, INNER, colu...  2.38 us

profile of v2, /device:TPU:1, one launch (start us, length us, event | category | flops | bytes accessed | tf_op | source)
XLA Modules:
  0.0 48.4 jit_solution(17654101575858450536)
XLA Ops:
  0.0 46.0 %average_step.1 = (bf16[4,16,4,2,32,128]{5,4,3,2,1,0:T(8,128)(2,1)S(1)}, bf16[16,256,512]{2,1,0:T(8,128)(2,1)S(1)}, bf16[16,256,256]{2,1,0:T(8,128)(2,1)S(1)}, f32[8,128]{1,0:T(8,128)S(1)}) custom-call(s32[1,4]{1,0:T(1,128)} %exps_hbm.1, s32[32,128]{1,0:T(8,128)} %bitcast.6, bf16[16,256,512]{2,1,0:T(8,128)(2,1)} %bitcast.4, bf16[16,256,512]{2,1,0:T(8,128)(2,1)} %bitcast.5), custom_call_target="tpu_custom_call" | custom-call | tf_op jit(solution)/shard_map/average_step/pallas_call | solution.py:426
  46.0 2.4 %finish_step.1 = bf16[16,256,512]{2,1,0:T(8,128)(2,1)} custom-call(bf16[4,16,4,2,32,128]{5,4,3,2,1,0:T(8,128)(2,1)S(1)} %get-tuple-element.9.gv, bf16[16,256,512]{2,1,0:T(8,128)(2,1)S(1)} %get-tuple-element.10.wv, bf16[16,256,256]{2,1,0:T(8,128)(2,1)S(1)} %get-tuple-element.11.hb, f32[8,128]{1,0:T(8,128)S(1)} %get-tuple-element.12.fac), custom_call_target="tpu_custom_call" | custom-call | tf_op jit(solution)/shard_map/finish_step/pallas_call | solution.py:473

commit v3 on v2

--- a/solution.py
+++ b/solution.py
@@ -14,16 +14,16 @@
 NG = 10
 CHUNKS = [(0, 0), (0, 1), (1, 0), (1, 1)]
 ORDER = [
-    "vp 0", "vp 3", "vp 2", "inner 1", "vp 1", "vo 0", "sz 0", "sd 0",
-    "vo 2", "sz 2", "vo 3", "vo 1", "tables 0", "sz 3", "sd 2", "a2s1 0",
-    "a1s2 0", "a1s2 3", "sz 1", "a1s2 2", "sd 3", "a2s1 2", "a1z 0", "sd 1",
-    "a2s2 0", "a2s1 3", "a1z 3", "a1s2 1", "a1z 2", "a2s2 2", "a2s1 1", "a2s2 3",
-    "fin 0", "a1z 1", "a2s2 1", "fin 2", "fin 3", "drain 0", "fin 1", "sum 0",
-    "g1 0", "g1 3", "gc1 3", "g2f 0", "g2f 3", "g2f 2", "g2q 3", "g1 1",
-    "g2q 0", "g1 2", "g2f 1", "sum 0", "g2q 2", "g2q 1", "g4 0", "g3 3",
-    "g3 0", "g4 3", "drain 0", "g4 2", "g3 1", "gc1 2", "g3 2", "g4 1",
-    "g5 0", "g5 2", "g5 3", "drain 0", "g6 0", "gc1 1", "g5 1", "gc1 0",
-    "g6 3", "g6 2", "drain 0", "g6 1", "sum 0",
+    "vp 0", "inner 1", "vp 2", "vp 1", "vo 0", "sz 0", "sd 0", "vp 3",
+    "vo 2", "vo 1", "sd 1", "sz 1", "vo 3", "a1s2 0", "sz 3", "sz 2",
+    "sd 2", "a1s2 1", "a2s1 0", "a1s2 3", "sd 3", "a1z 0", "a2s1 1", "a1s2 2",
+    "a2s1 3", "a1z 1", "a2s2 0", "a2s1 2", "a1z 3", "a2s2 1", "a1z 2", "a2s2 3",
+    "fin 0", "a2s2 2", "fin 1", "fin 3", "g1 0", "drain 0", "fin 2", "sum 0",
+    "g2f 0", "g1 3", "g2f 3", "g1 1", "g2q 0", "g2q 3", "g1 2", "g2f 2",
+    "g2f 1", "g3 0", "g2q 1", "sum 0", "g4 0", "g2q 2", "g5 0", "gc1 1",
+    "gc1 3", "g3 1", "g4 3", "gc1 0", "g3 3", "drain 0", "g3 2", "g4 2",
+    "gc1 2", "g5 1", "g4 1", "tables 0", "g5 3", "g5 2", "drain 0", "g6 3",
+    "g6 0", "g6 2", "drain 0", "g6 1", "sum 0",
 ]
 MESH = pl.DeviceIdType.MESH
 
@@ -69,11 +69,12 @@
     xpeer = {j: dev(x=xo[j]) for j in (1, 2, 3)}
     zpeer, cpeer, zcpeer = dev(z=oz), dev(c=oc), dev(z=oz, c=oc)
     rounds = [(x, list(xpeer.values())), (2 * z + c, [zpeer, cpeer, zcpeer])]
-    later = {}
+    later, later_y = {}, {}
     if nt > 1:
         turn = {j: (xo[j], lax.rem(yy + j, 4)) for j in (1, 2, 3)}
         turn[0] = (x, yy)
         plane = [dev(x=turn[i][0], yy=turn[j][1]) for i in range(4) for j in range(4) if i or j]
+        later_y = {j: [dev(x=turn[i][0], yy=turn[j][1]) for i in range(4)] for j in (1, 2, 3)}
         later = {j: [] for j in (1, 2, 3)}
         for j in later:
             there = lax.rem(zh + j, 4)
@@ -96,32 +97,36 @@
         if n == 0:
             small = [local(signs_hbm, signs), local(exps_hbm, exps)]
 
-    peers = rounds[0][1] + [zpeer, cpeer, zcpeer]
+    peers = [*xpeer.values(), zpeer, cpeer, zcpeer]
     barrier = pltpu.get_barrier_semaphore()
     for peer in peers:
         pl.semaphore_signal(barrier, inc=1, device_id=peer, device_id_type=MESH)
-    for j in later:
-
-        @pl.when(zh + j < 4)
-        def greet_later(j=j):
-            for peer in later[j]:
-                pl.semaphore_signal(barrier, inc=1, device_id=peer, device_id_type=MESH)
+    axes = [(yy, later_y), (zh, later)]
+    for at, others in axes:
+        for j in others:
+
+            @pl.when(at + j < 4)
+            def greet_later(others=others, j=j):
+                for peer in others[j]:
+                    pl.semaphore_signal(barrier, inc=1, device_id=peer, device_id_type=MESH)
 
     def enter():
-        pl.semaphore_wait(barrier, len(peers) + (4 * zh if nt > 1 else 0))
-        for j in later:
-
-            @pl.when(zh + j >= 4)
-            def answer_earlier(j=j):
-                for peer in later[j]:
-                    pl.semaphore_signal(entered, inc=1, device_id=peer, device_id_type=MESH)
-
-    def await_later():
+        pl.semaphore_wait(barrier, len(peers) + (4 * yy + 4 * zh if nt > 1 else 0))
+        for n, (at, others) in enumerate(axes):
+            for j in others:
+
+                @pl.when(at + j >= 4)
+                def answer_earlier(others=others, j=j, n=n):
+                    for peer in others[j]:
+                        pl.semaphore_signal(entered.at[n], inc=1, device_id=peer, device_id_type=MESH)
+
+    def await_later(n):
         if nt > 1:
-
-            @pl.when(zh < 3)
+            at = axes[n][0]
+
+            @pl.when(at < 3)
             def _():
-                pl.semaphore_wait(entered, 12 - 4 * zh)
+                pl.semaphore_wait(entered.at[n], 12 - 4 * at)
 
     sent = []
 
@@ -341,8 +346,7 @@
             return total
         slot, to = rounds[n]
         ar[n, slot] = total
-        if n == 1:
-            await_later()
+        await_later(n)
         ar_copies[:] = [remote(ar.at[n, slot], ar.at[n, slot], peer) for peer in to]
         return None
 
@@ -458,7 +462,7 @@
             pltpu.SemaphoreType.DMA((16,)),
             pltpu.SemaphoreType.DMA((n_copies,)),
             pltpu.SemaphoreType.DMA((n_copies,)),
-            pltpu.SemaphoreType.REGULAR,
+            pltpu.SemaphoreType.REGULAR((2,)),
         ],
         compiler_params=pltpu.CompilerParams(
             collective_id=0, has_side_effects=True, vmem_limit_bytes=30 * 2**20

time: 48.5 us -> 48.3 us (level)
  no operation moved by 1% of the time
where the time goes in v3:
time: 48.3 us; the launch traced here: 48.2 us
  Pallas kernels  48.2 us (100%)
    pallas_call x1, Pallas kernels, body(): pl.pallas_call(functools.partial(exchange, nt), out_shape=[vmem((4, OUTER...  45.8 us
    pallas_call x1, Pallas kernels, body(): pl.pallas_call(finish, out_shape=jax.ShapeDtypeStruct((OUTER, INNER, colu...  2.38 us

profile of v3, /device:TPU:1, one launch (start us, length us, event | category | flops | bytes accessed | tf_op | source)
XLA Modules:
  0.0 48.2 jit_solution(1876360994899192941)
XLA Ops:
  0.0 45.8 %average_step.1 = (bf16[4,16,4,2,32,128]{5,4,3,2,1,0:T(8,128)(2,1)S(1)}, bf16[16,256,512]{2,1,0:T(8,128)(2,1)S(1)}, bf16[16,256,256]{2,1,0:T(8,128)(2,1)S(1)}, f32[8,128]{1,0:T(8,128)S(1)}) custom-call(s32[1,4]{1,0:T(1,128)} %exps_hbm.1, s32[32,128]{1,0:T(8,128)} %bitcast.6, bf16[16,256,512]{2,1,0:T(8,128)(2,1)} %bitcast.4, bf16[16,256,512]{2,1,0:T(8,128)(2,1)} %bitcast.5), custom_call_target="tpu_custom_call" | custom-call | tf_op jit(solution)/shard_map/average_step/pallas_call | solution.py:430
  45.8 2.4 %finish_step.1 = bf16[16,256,512]{2,1,0:T(8,128)(2,1)} custom-call(bf16[4,16,4,2,32,128]{5,4,3,2,1,0:T(8,128)(2,1)S(1)} %get-tuple-element.9.gv, bf16[16,256,512]{2,1,0:T(8,128)(2,1)S(1)} %get-tuple-element.10.wv, bf16[16,256,256]{2,1,0:T(8,128)(2,1)S(1)} %get-tuple-element.11.hb, f32[8,128]{1,0:T(8,128)S(1)} %get-tuple-element.12.fac), custom_call_target="tpu_custom_call" | custom-call | tf_op jit(solution)/shard_map/finish_step/pallas_call | solution.py:477
